TPU v7x, 32 devices: a whole 2x2x4 slice. The times are simulated.
32 devices in a mesh: sec: 2 (over core), dom: 16 (over z, y, x).
Axes of the slice: x: 2, y: 2, z: 4, core: 2. Of those that a mesh axis runs over, the one named last changes fastest.
Arguments:
- state: float32 [3, 8, 262144], P(None, None, ('sec', 'dom')), may hold values from -6 to 6
- send_rows: int32 [524288], P(('sec', 'dom')), may hold values from 0 to 8191, as said below
- intersection_source: int32 [524288], P(('sec', 'dom')), may hold values from 0 to 16383, as said below
- intersection_weight: float32 [524288], P(('sec', 'dom')), may hold values from 0.1 to 1
- couple_rate: float32 [2, 3], P('sec'), may hold values from 0.2 to 0.8
- atm_metric: float32 [2, 131072], P(None, 'dom'), may hold values from 0.5 to 2
- wave_speed: float32 [8], replicated, may hold values from 0.5 to 2
- ocean_adjacent: int32 [6, 131072], P(None, 'dom'), may hold values from 0 to 9215, as said below
- ocean_edges: int32 [2, 8192], P(None, 'dom'), may hold values from 0 to 8191, as said below
- ocean_kappa: float32 [131072], P('dom'), may hold values from 0.02 to 0.15
Outputs:
- new_state: float32 [3, 8, 262144], P(None, None, ('sec', 'dom'))
Inputs may be any that keep to these rules, and one draw needn't show every extreme that they name: `send_rows`: the ocean's band runs across the atmosphere's, so every block intersects every block of the other section. Within a block, cut the rows into 16 strips of 512 rows by position across the band; the 1024 slots for peer p hold the rows of strips p, p + 1, ... (modulo 16), 2 strips in all, in an order drawn from the seed; so every row fills exactly 2 slots. `intersection_source`: in each block a permutation of all 16384 received slots; the entries 2 * r .. 2 * r + 1 belong to row r. `ocean_adjacent`: each cell's neighbours on a hexagonal grid in its block's own row order; values from 8192 on name rim slots (first the cells of the previous block's last column, then those of the next block's first column, by position across the band); a cell at the band's edge names itself for a missing neighbour. `ocean_edges`: ordered by position across the band.
All inputs are finite; a program needn't handle non-finite values.
Results may differ from a plain program's by a relative error of at most 0.0001.
Values sent between devices are 32-bit elements; how exact they have to be, the bound alone decides.
A program may use at most 128 MiB of HBM per device.

v0:
```python
import jax
import jax.numpy as jnp
import numpy as np
from jax import lax
from jax.sharding import PartitionSpec as P

INTERSECTIONS = 2
TIME_STEP = 0.05


def extended_2(shard, sides, width):
    for axis, dim in sides:
        size, length = (lax.axis_size(axis), shard.shape[dim])
        up = [(i, (i + 1) % size) for i in range(size)]
        down = [(j, i) for i, j in up]
        last = lax.slice_in_dim(shard, length - width, length, axis=dim)
        leading = lax.slice_in_dim(shard, 0, width, axis=dim)
        before = lax.ppermute(last, axis, up)
        after = lax.ppermute(leading, axis, down)
        shard = jnp.concatenate([before, shard, after], axis=dim)
    return shard


def gll_derivative():
    nodes = np.array([-1.0, -1.0 / np.sqrt(5.0), 1.0 / np.sqrt(5.0), 1.0])
    barycentric = np.array(
        [
            1.0 / np.prod([nodes[first] - nodes[second] for second in range(4) if second != first])
            for first in range(4)
        ]
    )
    matrix = np.zeros((4, 4))
    for first in range(4):
        for second in range(4):
            if first != second:
                matrix[first, second] = (
                    barycentric[second] / barycentric[first] / (nodes[first] - nodes[second])
                )
        matrix[first, first] = -np.sum(matrix[first])
    return jnp.asarray(matrix, jnp.float32)


def along_first(field, derivative):
    depth, across, along = field.shape
    grouped = field.reshape(depth, across // 4, 4, along)
    return jnp.einsum(
        "ij,lejy->leiy", derivative, grouped, precision=lax.Precision.HIGHEST
    ).reshape(field.shape)


def along_second(field, derivative):
    depth, across, along = field.shape
    grouped = field.reshape(depth, across, along // 4, 4)
    return jnp.einsum(
        "ij,lxej->lxei", derivative, grouped, precision=lax.Precision.HIGHEST
    ).reshape(field.shape)


def dycore(fields, metric_x, metric_y, speeds):
    derivative = gll_derivative()
    eastward, northward, geopotential = (fields[0], fields[1], fields[2])
    slope_x = metric_x * along_first(geopotential, derivative)
    slope_y = metric_y * along_second(geopotential, derivative)
    spread = metric_x * along_first(eastward, derivative) + metric_y * along_second(
        northward, derivative
    )
    return jnp.stack(
        [
            eastward - TIME_STEP * slope_x,
            northward - TIME_STEP * slope_y,
            geopotential - TIME_STEP * speeds[:, None, None] * spread,
        ]
    )


def average_first(fields, before, after):
    phase = (jnp.arange(fields.shape[2]) % 4)[:, None]
    return jnp.where(
        phase == 3, (fields + after) * 0.5, jnp.where(phase == 0, (fields + before) * 0.5, fields)
    )


def average_second(fields):
    along = fields.shape[3]
    position = jnp.arange(along)
    phase = position % 4
    after = jnp.roll(fields, -1, axis=3)
    before = jnp.roll(fields, 1, axis=3)
    joined_after = (phase == 3) & (position < along - 1)
    joined_before = (phase == 0) & (position > 0)
    return jnp.where(
        joined_after,
        (fields + after) * 0.5,
        jnp.where(joined_before, (fields + before) * 0.5, fields),
    )


def body(
    state,
    send_rows,
    intersection_source,
    intersection_weight,
    couple_rate,
    atm_metric,
    wave_speed,
    ocean_adjacent,
    ocean_edges,
    ocean_kappa,
):
    levels = state.shape[1]
    y_points = ocean_edges.shape[1]
    x_points = state.shape[2] // y_points
    section = lax.axis_index("sec")
    atmosphere = section == 0
    surface = state[:, levels - 1]
    outgoing = surface[:, send_rows]
    slot_count = outgoing.shape[1]
    blank = jnp.zeros_like(outgoing)
    spread_out = jnp.where(
        atmosphere,
        jnp.concatenate([blank, outgoing], axis=1),
        jnp.concatenate([outgoing, blank], axis=1),
    )
    arrived = lax.all_to_all(spread_out, ("sec", "dom"), split_axis=1, concat_axis=1, tiled=True)
    incoming = lax.dynamic_slice_in_dim(arrived, (1 - section) * slot_count, slot_count, 1)
    weights = intersection_weight.reshape(-1, INTERSECTIONS)
    values = incoming[:, intersection_source].reshape(3, -1, INTERSECTIONS)
    regrid = jnp.sum(values * weights, axis=-1) / jnp.sum(weights, axis=-1)
    metric = atm_metric.reshape(2, x_points, y_points)

    def advance(current):
        grid = current.reshape(3, levels, x_points, y_points)
        return dycore(grid, metric[0], metric[1], wave_speed).reshape(current.shape)

    def unchanged(current):
        return current

    segmented = lax.cond(atmosphere, advance, unchanged, state)
    positions = jnp.arange(y_points, dtype=jnp.int32)
    left_rows = jnp.where(atmosphere, positions, ocean_edges[0])
    right_rows = jnp.where(atmosphere, (x_points - 1) * y_points + positions, ocean_edges[1])
    border = jnp.stack([segmented[:, :, left_rows], segmented[:, :, right_rows]], axis=2)
    rimmed = extended_2(border, (("dom", 2),), 1)
    western = rimmed[:, :, 0]
    eastern = rimmed[:, :, 3]

    def finish_atmosphere(operands):
        current, west_side, east_side = operands
        grid = current.reshape(3, levels, x_points, y_points)
        padded = jnp.concatenate([west_side[:, :, None], grid, east_side[:, :, None]], axis=2)
        averaged = average_second(average_first(grid, padded[:, :, :-2], padded[:, :, 2:]))
        return averaged.reshape(current.shape)

    def sweep_ocean(operands):
        current, west_side, east_side = operands
        extended = jnp.concatenate([current, west_side, east_side], axis=2)
        summed = jnp.zeros_like(current)
        for neighbor in range(6):
            summed = summed + (extended[:, :, ocean_adjacent[neighbor]] - current)
        return current + ocean_kappa * summed

    updated = lax.cond(atmosphere, finish_atmosphere, sweep_ocean, (segmented, western, eastern))
    rates = couple_rate[0][:, None]
    surface_top = updated[:, levels - 1]
    surface_top = surface_top + rates * (regrid - surface_top)
    return updated.at[:, levels - 1].set(surface_top)


def solution(mesh):
    in_specs = (
        P(None, None, ("sec", "dom")),
        P(("sec", "dom")),
        P(("sec", "dom")),
        P(("sec", "dom")),
        P("sec", None),
        P(None, "dom"),
        P(),
        P(None, "dom"),
        P(None, "dom"),
        P("dom"),
    )
    out_specs = P(None, None, ("sec", "dom"))
    return jax.shard_map(body, mesh=mesh, in_specs=in_specs, out_specs=out_specs, check_vma=False)
```

profile of v0, /device:TPU:1, one launch (start us, length us, event | category | flops | bytes accessed | tf_op | source)
XLA Modules:
  0.0 745.3 jit_solution(7190524143693755592)
XLA Ops:
  1.2 2.6 copy.190
  4.7 56.6 %gather_fusion.8 = f32[16384,3]{1,0:T(8,128)} fusion(f32[3,8192]{0,1:T(8,128)} %bitcast.117, s32[16384]{0:T(1024)S(1)} %fusion.26), kind=kCustom, calls=%fused_computation.8 | custom fusion | bytes 458752 | tf_op jit(solution)/shard_map/gather | solution.py:116
  61.4 16.0 %pad_select_fusion = f32[3,32768]{0,1:T(8,128)} fusion(f32[3,16384]{0,1:T(8,128)} %bitcast.119, pred[]{:T(512)S(6)} %eq.33), kind=kLoop, calls=%fused_computation.75 | loop fusion | flops 98304 | bytes 589825 | tf_op jit(solution)/shard_map/jit(_where)/select_n | solution.py:119
  77.4 9.9 %copy.184 = f32[3,32,1024]{2,0,1:T(4,128)} copy(f32[3,32,1024]{0,2,1:T(8,128)} %bitcast.109) | data formatting | bytes 786432 | tf_op jit(solution)/shard_map/all_to_all | solution.py:124
  87.3 7.2 all-to-all-start
  94.5 10.6 %copy.176 = f32[3,8,8192]{1,0,2:T(4,128)} copy(f32[3,8,8192]{2,1,0:T(8,128)S(1)} %get-tuple-element.175) | data formatting | bytes 1572864 | tf_op jit(solution)/shard_map/cond | solution.py:138
  105.1 7.3 gather_fusion.7
  112.6 5.3 collective-permute-start.1
  117.9 7.3 gather_fusion.6
  125.6 5.5 mul.165
  131.1 3.3 reduce_sum.22
  134.5 482.6 %conditional.3 = (f32[3,8,8192]{2,1,0:T(8,128)}) conditional(s32[]{:T(128)} %convert_element_type.4, (f32[8192]{0:T(1024)S(1)}, f32[3,8,1,512]{3,1,2,0:T(8,128)S(1)}, f32[3,8,1,512]{3,1,2,0:T(8,128)S(1)}, f32[3,8,8192]{2,1,0:T(8,128)S(1)}, s32[6,8192]{1,0:T(8,128)S(1)}) %tuple.75, (f32[3,8,8192]{2,1,0:T(8,128)S(1)}, f32[3,8,1,512]{3,1,2,0:T(8,128)S(1)}, ...), branch_computations={%region_2.3_spmd, %region_3.4_spmd} | conditional | flops 4724864 | bytes 29720584 | solution.py:162
  134.5 11.9 %copy.164 = f32[3,8,9216]{1,0,2:T(4,128)} copy(f32[3,8,9216]{2,1,0:T(8,128)S(1)} %pad_maximum_fusion.3) | data formatting | bytes 1769472 | tf_op jit(solution)/shard_map/cond/branch_0_fun/concatenate | solution.py:156
  146.7 65.8 %gather_fusion = f32[8192,3,8]{2,1,0:T(4,128)} fusion(f32[3,8,9216]{1,0,2:T(4,128)} %copy.164, s32[8192]{0:T(1024)S(1)} %broadcast_clamp_fusion.5), kind=kCustom, calls=%fused_computation | custom fusion | bytes 1605632 | tf_op jit(solution)/shard_map/cond/branch_0_fun/gather | solution.py:159
  212.5 11.7 %copy.165 = f32[8192,3,8]{0,2,1:T(8,128)S(1)} copy(f32[8192,3,8]{2,1,0:T(4,128)} %gather_fusion) | data formatting | bytes 1572864 | tf_op jit(solution)/shard_map/cond/branch_0_fun/gather | solution.py:159
  224.2 65.8 %gather_fusion.1 = f32[8192,3,8]{2,1,0:T(4,128)} fusion(f32[3,8,9216]{1,0,2:T(4,128)} %copy.164, s32[8192]{0:T(1024)S(1)} %broadcast_clamp_fusion.4), kind=kCustom, calls=%fused_computation.1 | custom fusion | bytes 1605632 | tf_op jit(solution)/shard_map/cond/branch_0_fun/gather | solution.py:159
  290.0 11.7 %copy.167 = f32[8192,3,8]{0,2,1:T(8,128)S(1)} copy(f32[8192,3,8]{2,1,0:T(4,128)} %gather_fusion.1) | data formatting | bytes 1572864 | tf_op jit(solution)/shard_map/cond/branch_0_fun/gather | solution.py:159
  301.7 65.8 %gather_fusion.2 = f32[8192,3,8]{2,1,0:T(4,128)} fusion(f32[3,8,9216]{1,0,2:T(4,128)} %copy.164, s32[8192]{0:T(1024)S(1)} %broadcast_clamp_fusion.3), kind=kCustom, calls=%fused_computation.2 | custom fusion | bytes 1605632 | tf_op jit(solution)/shard_map/cond/branch_0_fun/gather | solution.py:159
  367.6 11.7 %copy.169 = f32[8192,3,8]{0,2,1:T(8,128)S(1)} copy(f32[8192,3,8]{2,1,0:T(4,128)} %gather_fusion.2) | data formatting | bytes 1572864 | tf_op jit(solution)/shard_map/cond/branch_0_fun/gather | solution.py:159
  379.2 65.8 %gather_fusion.3 = f32[8192,3,8]{2,1,0:T(4,128)} fusion(f32[3,8,9216]{1,0,2:T(4,128)} %copy.164, s32[8192]{0:T(1024)S(1)} %broadcast_clamp_fusion.2), kind=kCustom, calls=%fused_computation.3 | custom fusion | bytes 1605632 | tf_op jit(solution)/shard_map/cond/branch_0_fun/gather | solution.py:159
  445.1 12.5 %copy.171 = f32[8192,3,8]{0,2,1:T(8,128)} copy(f32[8192,3,8]{2,1,0:T(4,128)} %gather_fusion.3) | data formatting | bytes 1572864 | tf_op jit(solution)/shard_map/cond/branch_0_fun/gather | solution.py:159
  457.6 65.8 %gather_fusion.4 = f32[8192,3,8]{2,1,0:T(4,128)} fusion(f32[3,8,9216]{1,0,2:T(4,128)} %copy.164, s32[8192]{0:T(1024)S(1)} %broadcast_clamp_fusion.1), kind=kCustom, calls=%fused_computation.4 | custom fusion | bytes 1605632 | tf_op jit(solution)/shard_map/cond/branch_0_fun/gather | solution.py:159
  523.4 12.5 %copy.173 = f32[8192,3,8]{0,2,1:T(8,128)} copy(f32[8192,3,8]{2,1,0:T(4,128)} %gather_fusion.4) | data formatting | bytes 1572864 | tf_op jit(solution)/shard_map/cond/branch_0_fun/gather | solution.py:159
  535.9 65.8 %gather_fusion.5 = f32[8192,3,8]{2,1,0:T(4,128)} fusion(f32[3,8,9216]{1,0,2:T(4,128)} %copy.164, s32[8192]{0:T(1024)S(1)} %broadcast_clamp_fusion), kind=kCustom, calls=%fused_computation.5 | custom fusion | bytes 1605632 | tf_op jit(solution)/shard_map/cond/branch_0_fun/gather | solution.py:159
  601.8 12.5 %copy.175 = f32[8192,3,8]{0,2,1:T(8,128)} copy(f32[8192,3,8]{2,1,0:T(4,128)} %gather_fusion.5) | data formatting | bytes 1572864 | tf_op jit(solution)/shard_map/cond/branch_0_fun/gather | solution.py:159
  614.3 2.8 fusion.21
  618.3 9.2 %copy.185 = f32[3,32,1024]{0,2,1:T(8,128)} copy(f32[3,32,1024]{2,0,1:T(4,128)} %all-to-all-done) | data formatting | bytes 786432 | tf_op jit(solution)/shard_map/all_to_all | solution.py:124
  627.5 5.7 constant_dynamic-slice_fusion
  633.3 57.9 %gather_fusion.9 = f32[16384,3]{1,0:T(8,128)} fusion(f32[3,16384]{0,1:T(8,128)} %constant_dynamic-slice_fusion, s32[16384]{0:T(1024)S(1)} %fusion.27), kind=kCustom, calls=%fused_computation.9 | custom fusion | bytes 458752 | tf_op jit(solution)/shard_map/gather | solution.py:127
  691.2 48.0 %multiply_reduce_fusion = f32[3,8192]{0,1:T(8,128)} fusion(f32[3,8192,2]{0,2,1:T(2,128)} %bitcast.118, f32[8192,2]{1,0:T(8,128)} %mul.165), kind=kLoop, calls=%fused_computation.76 | loop fusion | flops 73728 | bytes 360448 | tf_op jit(solution)/shard_map/reduce_sum | solution.py:128
  739.2 2.8 copy.186
  742.2 3.0 scatter.4
  (41 shorter events, 4.5 us)
Async XLA Ops:
  61.4 33.1 %copy-start.6 = (s32[2,512]{1,0:T(2,128)S(1)}, s32[2,512]{1,0:T(2,128)}, u32[]{:S(2)}) copy-start(s32[2,512]{1,0:T(2,128)} %param.25) | copy-start | bytes 12292
  61.4 33.1 %copy-start.2 = (f32[2,8192]{1,0:T(2,128)S(1)}, f32[2,8192]{1,0:T(2,128)}, u32[]{:S(2)}) copy-start(f32[2,8192]{1,0:T(2,128)} %param.22) | copy-start | bytes 196612
  61.4 33.1 %copy-start.8 = (f32[8]{0:T(128)S(1)}, f32[8]{0:T(128)}, u32[]{:S(2)}) copy-start(f32[8]{0:T(128)} %param.23) | copy-start | bytes 100
  87.3 531.1 %all-to-all-start = ((f32[3,32,1024]{2,0,1:T(4,128)}), f32[3,32,1024]{2,0,1:T(4,128)}, u32[]{:S(2)}, u32[]{:S(2)}) async-start(f32[3,32,1024]{2,0,1:T(4,128)} %copy.184), calls=%async_computation | async-start | bytes 1048576 | tf_op jit(solution)/shard_map/all_to_all | solution.py:124
  94.5 31.0 %copy-start.3 = (s32[16384]{0:T(1024)S(1)}, s32[16384]{0:T(1024)}, u32[]{:S(2)}) copy-start(s32[16384]{0:T(1024)} %param.19) | copy-start | bytes 196612
  94.5 31.1 %copy-start.1 = (f32[16384]{0:T(1024)S(1)}, f32[16384]{0:T(1024)}, u32[]{:S(2)}) copy-start(f32[16384]{0:T(1024)} %param.20) | copy-start | bytes 196612
  94.5 39.9 %copy-start = (s32[6,8192]{1,0:T(8,128)S(1)}, s32[6,8192]{1,0:T(8,128)}, u32[]{:S(2)}) copy-start(s32[6,8192]{1,0:T(8,128)} %param.24) | copy-start | bytes 589828
  94.5 39.9 %copy-start.4 = (f32[8192]{0:T(1024)S(1)}, f32[8192]{0:T(1024)}, u32[]{:S(2)}) copy-start(f32[8192]{0:T(1024)} %param.26) | copy-start | bytes 98308
  112.6 21.8 %collective-permute-start.1 = (f32[3,8,1,512]{3,1,2,0:T(8,128)S(1)}, f32[3,8,1,512]{3,1,2,0:T(8,128)S(1)}, u32[]{:S(2)}, u32[]{:S(2)}) collective-permute-start(f32[3,8,1,512]{3,1,2,0:T(8,128)S(1)} %copy.179), channel_id=1, source_target_pairs={{1,0},{2,1},{3,2},{4,3},{5,4},{6,5},{7,6},{8,7},{9,8},{10,9},{11,1... | collective-permute-start | bytes 147464 | tf_op jit(solution)/shard_map/ppermute | solution.py:19
  125.5 9.0 %collective-permute-start = (f32[3,8,1,512]{3,1,2,0:T(8,128)S(1)}, f32[3,8,1,512]{3,1,2,0:T(8,128)S(1)}, u32[]{:S(2)}, u32[]{:S(2)}) collective-permute-start(f32[3,8,1,512]{3,1,2,0:T(8,128)S(1)} %copy.177), channel_id=1, source_target_pairs={{0,1},{1,2},{2,3},{3,4},{4,5},{5,6},{6,7},{7,8},{8,9},{9,10},{10,1... | collective-permute-start | bytes 147464 | tf_op jit(solution)/shard_map/ppermute | solution.py:18
  627.5 114.5 %copy-start.7 = (f32[1,3]{1,0:T(1,128)S(1)}, f32[1,3]{1,0:T(1,128)}, u32[]{:S(2)}) copy-start(f32[1,3]{1,0:T(1,128)} %param.21) | copy-start | bytes 40
where the time goes:
time: 748 us; the launch traced here: 745 us
  local copies, waits for them, and re-layouts  661 us (88%)
  other arithmetic  71.5 us (10%)
  starting transfers between devices  12.5 us (2%)
    gather x12, local copies, waits for them, and re-layouts, sweep_ocean(): summed = summed + (extended[:, :, ocean_adjacent[neighbor]] - current)  468 us
    gather x1, local copies, waits for them, and re-layouts, body(): values = incoming[:, intersection_source].reshape(3, -1, INTERSECTIONS)  57.9 us
    gather x1, local copies, waits for them, and re-layouts, body(): outgoing = surface[:, send_rows]  56.6 us
    reduce_sum x2, other arithmetic, body(): regrid = jnp.sum(values * weights, axis=-1) / jnp.sum(weights, axis=-1)  51.3 us
    all_to_all x2, local copies, waits for them, and re-layouts, body(): lax.all_to_all(spread_out, ('sec', 'dom'), split_axis=1, concat_axis=1, t...  19.1 us
    select_n x1, other arithmetic, body(): jnp.where(atmosphere, jnp.concatenate([blank, outgoing], axis=1), jnp.con...  16 us
  transfers between devices with their start and end apart: 3, of which 0 were waited for; matrix products, arithmetic and copies ran while one was open for 70% of the time, Pallas kernels for 0%

commit v1 on v0

--- a/solution.py
+++ b/solution.py
@@ -121,7 +121,10 @@
         jnp.concatenate([blank, outgoing], axis=1),
         jnp.concatenate([outgoing, blank], axis=1),
     )
-    arrived = lax.all_to_all(spread_out, ("sec", "dom"), split_axis=1, concat_axis=1, tiled=True)
+    n_dev = lax.axis_size(("sec", "dom"))
+    pieces = jnp.stack(jnp.split(spread_out, n_dev, axis=1), axis=0)
+    pieces = lax.all_to_all(pieces, ("sec", "dom"), split_axis=0, concat_axis=0)
+    arrived = jnp.concatenate(pieces, axis=1)
     incoming = lax.dynamic_slice_in_dim(arrived, (1 - section) * slot_count, slot_count, 1)
     weights = intersection_weight.reshape(-1, INTERSECTIONS)
     values = incoming[:, intersection_source].reshape(3, -1, INTERSECTIONS)

time: 748 us -> 772 us (1.032)
  local copies, waits for them, and re-layouts: 661 us -> 690 us
    unnamed x18 -> x47, local copies, waits for them, and re-layouts: 3.79 us -> 29.9 us
    all_to_all x2 -> x0, local copies, waits for them, and re-layouts: 19.1 us -> none  [body(): lax.all_to_all(spread_out, ('sec', 'dom'), split_axis=1, concat_axis=1, t...]
    another operation x0 -> x2, local copies, waits for them, and re-layouts: none -> 10.7 us  [body(): pieces = jnp.stack(jnp.split(spread_out, n_dev, axis=1), axis=0)]
    reshape x0 -> x1, local copies, waits for them, and re-layouts: none -> 9.13 us  [body(): arrived = jnp.concatenate(pieces, axis=1)]
  transfers between devices with their start and end apart: 3 -> 3, of which waited for: 0 -> 0; matrix products, arithmetic and copies ran while one was open for 70% -> 67% of each run, Pallas kernels for 0% -> 0%
where the time goes in v1:
time: 772 us; the launch traced here: 770 us
  local copies, waits for them, and re-layouts  690 us (89%)
  other arithmetic  67.5 us (9%)
  starting transfers between devices  12.3 us (2%)
    gather x12, local copies, waits for them, and re-layouts, sweep_ocean(): summed = summed + (extended[:, :, ocean_adjacent[neighbor]] - current)  469 us
    gather x1, local copies, waits for them, and re-layouts, body(): values = incoming[:, intersection_source].reshape(3, -1, INTERSECTIONS)  58.1 us
    gather x1, local copies, waits for them, and re-layouts, body(): outgoing = surface[:, send_rows]  57 us
    reduce_sum x2, other arithmetic, body(): regrid = jnp.sum(values * weights, axis=-1) / jnp.sum(weights, axis=-1)  51.3 us
    unnamed x47, local copies, waits for them, and re-layouts  29.9 us
  transfers between devices with their start and end apart: 3, of which 0 were waited for; matrix products, arithmetic and copies ran while one was open for 67% of the time, Pallas kernels for 0%

profile of v1, /device:TPU:1, one launch (start us, length us, event | category | flops | bytes accessed | tf_op | source)
XLA Modules:
  0.0 769.9 jit_solution(2372373087660765375)
XLA Ops:
  1.2 2.6 copy.254
  4.8 57.0 %gather_fusion.8 = f32[16384,3]{1,0:T(8,128)} fusion(f32[3,8192]{0,1:T(8,128)} %bitcast.244, s32[16384]{0:T(1024)S(1)} %get-tuple-element.175), kind=kCustom, calls=%fused_computation.8 | custom fusion | bytes 458752 | tf_op jit(solution)/shard_map/gather | solution.py:116
  61.7 12.0 %pad_select_fusion = f32[3,32768]{0,1:T(8,128)S(1)} fusion(f32[3,16384]{0,1:T(8,128)} %bitcast.246, pred[]{:T(512)S(6)} %eq.33), kind=kLoop, calls=%fused_computation.75 | loop fusion | flops 98304 | bytes 589825 | tf_op jit(solution)/shard_map/jit(_where)/select_n | solution.py:119
  100.6 9.9 %copy.248 = f32[32,3,1024]{2,1,0:T(4,128)} copy(f32[32,3,1024]{1,2,0:T(8,128)} %fusion.26) | data formatting | bytes 786432 | tf_op jit(solution)/shard_map/stack | solution.py:125
  110.5 7.2 all-to-all-start
  117.9 10.6 %copy.240 = f32[3,8,8192]{1,0,2:T(4,128)} copy(f32[3,8,8192]{2,1,0:T(8,128)S(1)} %get-tuple-element.179) | data formatting | bytes 1572864 | tf_op jit(solution)/shard_map/cond | solution.py:141
  128.5 7.3 gather_fusion.7
  136.1 5.1 collective-permute-start.1
  141.2 7.3 gather_fusion.6
  148.8 5.5 mul.165
  154.3 3.3 reduce_sum.22
  157.7 483.8 %conditional.3 = (f32[3,8,8192]{2,1,0:T(8,128)}) conditional(s32[]{:T(128)} %convert_element_type.4, (f32[8192]{0:T(1024)S(1)}, f32[3,8,1,512]{3,1,2,0:T(8,128)S(1)}, f32[3,8,1,512]{3,1,2,0:T(8,128)S(1)}, f32[3,8,8192]{2,1,0:T(8,128)S(1)}, s32[6,8192]{1,0:T(8,128)S(1)}) %tuple.77, (f32[3,8,8192]{2,1,0:T(8,128)S(1)}, f32[3,8,1,512]{3,1,2,0:T(8,128)S(1)}, ...), branch_computations={%region_2.3_spmd, %region_3.4_spmd} | conditional | flops 4724864 | bytes 29720584 | solution.py:165
  157.8 11.9 %copy.228 = f32[3,8,9216]{1,0,2:T(4,128)} copy(f32[3,8,9216]{2,1,0:T(8,128)S(1)} %pad_maximum_fusion.3) | data formatting | bytes 1769472 | tf_op jit(solution)/shard_map/cond/branch_0_fun/concatenate | solution.py:159
  169.9 66.0 %gather_fusion = f32[8192,3,8]{2,1,0:T(4,128)} fusion(f32[3,8,9216]{1,0,2:T(4,128)} %copy.228, s32[8192]{0:T(1024)S(1)} %broadcast_clamp_fusion.5), kind=kCustom, calls=%fused_computation | custom fusion | bytes 1605632 | tf_op jit(solution)/shard_map/cond/branch_0_fun/gather | solution.py:162
  235.9 11.7 %copy.229 = f32[8192,3,8]{0,2,1:T(8,128)S(1)} copy(f32[8192,3,8]{2,1,0:T(4,128)} %gather_fusion) | data formatting | bytes 1572864 | tf_op jit(solution)/shard_map/cond/branch_0_fun/gather | solution.py:162
  247.6 66.0 %gather_fusion.1 = f32[8192,3,8]{2,1,0:T(4,128)} fusion(f32[3,8,9216]{1,0,2:T(4,128)} %copy.228, s32[8192]{0:T(1024)S(1)} %broadcast_clamp_fusion.4), kind=kCustom, calls=%fused_computation.1 | custom fusion | bytes 1605632 | tf_op jit(solution)/shard_map/cond/branch_0_fun/gather | solution.py:162
  313.7 11.7 %copy.231 = f32[8192,3,8]{0,2,1:T(8,128)S(1)} copy(f32[8192,3,8]{2,1,0:T(4,128)} %gather_fusion.1) | data formatting | bytes 1572864 | tf_op jit(solution)/shard_map/cond/branch_0_fun/gather | solution.py:162
  325.3 66.0 %gather_fusion.2 = f32[8192,3,8]{2,1,0:T(4,128)} fusion(f32[3,8,9216]{1,0,2:T(4,128)} %copy.228, s32[8192]{0:T(1024)S(1)} %broadcast_clamp_fusion.3), kind=kCustom, calls=%fused_computation.2 | custom fusion | bytes 1605632 | tf_op jit(solution)/shard_map/cond/branch_0_fun/gather | solution.py:162
  391.4 11.7 %copy.233 = f32[8192,3,8]{0,2,1:T(8,128)S(1)} copy(f32[8192,3,8]{2,1,0:T(4,128)} %gather_fusion.2) | data formatting | bytes 1572864 | tf_op jit(solution)/shard_map/cond/branch_0_fun/gather | solution.py:162
  403.1 66.0 %gather_fusion.3 = f32[8192,3,8]{2,1,0:T(4,128)} fusion(f32[3,8,9216]{1,0,2:T(4,128)} %copy.228, s32[8192]{0:T(1024)S(1)} %broadcast_clamp_fusion.2), kind=kCustom, calls=%fused_computation.3 | custom fusion | bytes 1605632 | tf_op jit(solution)/shard_map/cond/branch_0_fun/gather | solution.py:162
  469.1 12.5 %copy.235 = f32[8192,3,8]{0,2,1:T(8,128)} copy(f32[8192,3,8]{2,1,0:T(4,128)} %gather_fusion.3) | data formatting | bytes 1572864 | tf_op jit(solution)/shard_map/cond/branch_0_fun/gather | solution.py:162
  481.6 66.0 %gather_fusion.4 = f32[8192,3,8]{2,1,0:T(4,128)} fusion(f32[3,8,9216]{1,0,2:T(4,128)} %copy.228, s32[8192]{0:T(1024)S(1)} %broadcast_clamp_fusion.1), kind=kCustom, calls=%fused_computation.4 | custom fusion | bytes 1605632 | tf_op jit(solution)/shard_map/cond/branch_0_fun/gather | solution.py:162
  547.7 12.5 %copy.237 = f32[8192,3,8]{0,2,1:T(8,128)} copy(f32[8192,3,8]{2,1,0:T(4,128)} %gather_fusion.4) | data formatting | bytes 1572864 | tf_op jit(solution)/shard_map/cond/branch_0_fun/gather | solution.py:162
  560.2 66.0 %gather_fusion.5 = f32[8192,3,8]{2,1,0:T(4,128)} fusion(f32[3,8,9216]{1,0,2:T(4,128)} %copy.228, s32[8192]{0:T(1024)S(1)} %broadcast_clamp_fusion), kind=kCustom, calls=%fused_computation.5 | custom fusion | bytes 1605632 | tf_op jit(solution)/shard_map/cond/branch_0_fun/gather | solution.py:162
  626.2 12.5 %copy.239 = f32[8192,3,8]{0,2,1:T(8,128)} copy(f32[8192,3,8]{2,1,0:T(4,128)} %gather_fusion.5) | data formatting | bytes 1572864 | tf_op jit(solution)/shard_map/cond/branch_0_fun/gather | solution.py:162
  638.7 2.8 fusion.21
  642.8 9.1 %copy.249 = f32[3,32,1024]{0,2,1:T(8,128)} copy(f32[3,32,1024]{2,0,1:T(4,128)} %bitcast.67) | data formatting | bytes 786432 | tf_op jit(solution)/shard_map/reshape | solution.py:127
  651.9 5.7 constant_dynamic-slice_fusion
  657.6 58.1 %gather_fusion.9 = f32[16384,3]{1,0:T(8,128)} fusion(f32[3,16384]{0,1:T(8,128)} %constant_dynamic-slice_fusion, s32[16384]{0:T(1024)S(1)} %get-tuple-element.176), kind=kCustom, calls=%fused_computation.9 | custom fusion | bytes 458752 | tf_op jit(solution)/shard_map/gather | solution.py:130
  715.8 48.0 %multiply_reduce_fusion = f32[3,8192]{0,1:T(8,128)} fusion(f32[3,8192,2]{0,2,1:T(2,128)} %bitcast.245, f32[8192,2]{1,0:T(8,128)} %mul.165), kind=kLoop, calls=%fused_computation.76 | loop fusion | flops 73728 | bytes 360448 | tf_op jit(solution)/shard_map/reduce_sum | solution.py:131
  763.8 2.8 copy.250
  766.9 3.0 scatter.4
  (69 shorter events, 31.6 us)
Async XLA Ops:
  88.8 28.9 %copy-start.2 = (f32[2,8192]{1,0:T(2,128)S(1)}, f32[2,8192]{1,0:T(2,128)}, u32[]{:S(2)}) copy-start(f32[2,8192]{1,0:T(2,128)} %param.22) | copy-start | bytes 196612
  88.8 28.9 %copy-start.7 = (f32[8]{0:T(128)S(1)}, f32[8]{0:T(128)}, u32[]{:S(2)}) copy-start(f32[8]{0:T(128)} %param.23) | copy-start | bytes 100
  110.5 532.2 %all-to-all-start = ((f32[32,3,1024]{2,1,0:T(4,128)}), f32[32,3,1024]{2,1,0:T(4,128)}, u32[]{:S(2)}, u32[]{:S(2)}) async-start(f32[32,3,1024]{2,1,0:T(4,128)} %copy.248), calls=%async_computation | async-start | bytes 1048576 | tf_op jit(solution)/shard_map/all_to_all | solution.py:126
  117.9 10.6 %copy-start.5 = (s32[2,512]{1,0:T(2,128)S(1)}, s32[2,512]{1,0:T(2,128)}, u32[]{:S(2)}) copy-start(s32[2,512]{1,0:T(2,128)} %param.25) | copy-start | bytes 12292
  117.9 30.9 %copy-start.1 = (f32[16384]{0:T(1024)S(1)}, f32[16384]{0:T(1024)}, u32[]{:S(2)}) copy-start(f32[16384]{0:T(1024)} %param.20) | copy-start | bytes 196612
  117.9 39.8 %copy-start = (s32[6,8192]{1,0:T(8,128)S(1)}, s32[6,8192]{1,0:T(8,128)}, u32[]{:S(2)}) copy-start(s32[6,8192]{1,0:T(8,128)} %param.24) | copy-start | bytes 589828
  117.9 39.8 %copy-start.3 = (f32[8192]{0:T(1024)S(1)}, f32[8192]{0:T(1024)}, u32[]{:S(2)}) copy-start(f32[8192]{0:T(1024)} %param.26) | copy-start | bytes 98308
  136.1 21.6 %collective-permute-start.1 = (f32[3,8,1,512]{3,1,2,0:T(8,128)S(1)}, f32[3,8,1,512]{3,1,2,0:T(8,128)S(1)}, u32[]{:S(2)}, u32[]{:S(2)}) collective-permute-start(f32[3,8,1,512]{3,1,2,0:T(8,128)S(1)} %copy.243), channel_id=1, source_target_pairs={{1,0},{2,1},{3,2},{4,3},{5,4},{6,5},{7,6},{8,7},{9,8},{10,9},{11,1... | collective-permute-start | bytes 147464 | tf_op jit(solution)/shard_map/ppermute | solution.py:19
  148.7 8.9 %collective-permute-start = (f32[3,8,1,512]{3,1,2,0:T(8,128)S(1)}, f32[3,8,1,512]{3,1,2,0:T(8,128)S(1)}, u32[]{:S(2)}, u32[]{:S(2)}) collective-permute-start(f32[3,8,1,512]{3,1,2,0:T(8,128)S(1)} %copy.241), channel_id=1, source_target_pairs={{0,1},{1,2},{2,3},{3,4},{4,5},{5,6},{6,7},{7,8},{8,9},{9,10},{10,1... | collective-permute-start | bytes 147464 | tf_op jit(solution)/shard_map/ppermute | solution.py:18
  651.9 114.7 %copy-start.6 = (f32[1,3]{1,0:T(1,128)S(1)}, f32[1,3]{1,0:T(1,128)}, u32[]{:S(2)}) copy-start(f32[1,3]{1,0:T(1,128)} %param.21) | copy-start | bytes 40
